TPU v7x, 128 devices: a whole 4x4x4 slice. The times are simulated.
128 devices in a mesh: frame: 8 (over y, core), elem: 16 (over x, z).
Axes of the slice: x: 4, y: 4, z: 4, core: 2. Of those that a mesh axis runs over, the one named last changes fastest.
Arguments:
- strain_db: bfloat16 [8, 2048, 25, 6, 256], P('frame', 'elem'), may hold values from -6 to 6
- owner: int32 [8, 16384, 1], P(None, ('frame', 'elem')), may hold values from 0 to 15; in each aligned block of 128 rows (0 to 127, 128 to 255, ..., all dimensions but the last counted through in order) at most 12 rows name the same one
- local_elem: int32 [8, 16384], P(None, ('frame', 'elem')), may hold values from 0 to 127
- lattice: int32 [8, 2, 16384], P(None, None, ('frame', 'elem')), may hold values from 0 to 64
- pair_source: int32 [16], replicated, may hold values from 0 to 3
- pair_receiver: int32 [16], replicated, may hold values from 0 to 3
- filters: float32 [64, 64], replicated, may hold values from 0 to 1
Outputs:
- kernel: float32 [16, 64, 16384], P(None, None, ('frame', 'elem'))
Inputs may be any that keep to these rules, and one draw needn't show every extreme that they name: `owner`: within one group, the cells of one device name any elem index at most 12 times, and some index reaches that.
All inputs are finite; a program needn't handle non-finite values.
Results may differ from a plain program's by a relative error of at most 0.0068.
Values may be sent and summed in bfloat16 or wider, within the bound.
A program may use at most 128 MiB of HBM per device.

v0:
```python
import math

import jax
import jax.numpy as jnp
from jax import lax
from jax.sharding import PartitionSpec as P

C = 6
T_SIZE = 256
NF = 64
Q = 64


gll_nodes = [-1.0, -math.sqrt(3.0 / 7.0), 0.0, math.sqrt(3.0 / 7.0), 1.0]


def lagrange(coord):
    values = []
    for i in range(5):
        term = jnp.ones_like(coord)
        for j in range(5):
            if j != i:
                term = term * (coord - gll_nodes[j]) / (gll_nodes[i] - gll_nodes[j])
        values.append(term)
    return jnp.stack(values, axis=-1)


def basis_weights(steps_x, steps_y):
    coord_x = -1.0 + 2.0 * steps_x.astype(jnp.float32) / Q
    coord_y = -1.0 + 2.0 * steps_y.astype(jnp.float32) / Q
    along_x = lagrange(coord_x)
    along_y = lagrange(coord_y)
    weights = along_x[..., :, None] * along_y[..., None, :]
    return weights.reshape(steps_x.shape + (25,)).astype(jnp.bfloat16)


def dft_table():
    times = jnp.arange(T_SIZE, dtype=jnp.int32)[:, None]
    bins = jnp.arange(NF, dtype=jnp.int32)[None, :]
    phase = (times * bins % T_SIZE).astype(jnp.float32) * (2.0 * math.pi / T_SIZE)
    scale = 1.0 / math.sqrt(T_SIZE)
    return jnp.concatenate([jnp.cos(phase) * scale, -jnp.sin(phase) * scale], axis=1)


def transform(trace):
    table = dft_table()
    return jnp.dot(trace.astype(jnp.float32), table, precision=lax.Precision.HIGHEST).astype(
        jnp.bfloat16
    )


def interpolate(requests, table_db, elem_count):
    elem_req, steps_x, steps_y = requests
    shape = elem_req.shape
    flat_elem = elem_req.reshape(-1)
    weights = basis_weights(steps_x.reshape(-1), steps_y.reshape(-1))
    hit = (flat_elem[:, None] == jnp.arange(elem_count, dtype=jnp.int32)[None, :]).astype(
        jnp.bfloat16
    )
    dense = (hit[:, :, None] * weights[:, None, :]).reshape(flat_elem.shape[0], elem_count * 25)
    trace = jnp.dot(dense, table_db, preferred_element_type=jnp.float32).astype(jnp.bfloat16)
    trace = trace.reshape(shape + (C, T_SIZE))
    return trace


def local(strain_db, owner, local_elem, lattice, pair_source, pair_receiver, filters):
    groups, cells, _ = owner.shape
    n_elem = lax.axis_size("elem")
    slots = max(2, 3 * cells // (2 * n_elem))
    elem_count = strain_db.shape[1]
    table_db = strain_db.reshape(elem_count * 25, C * T_SIZE)
    target = owner[:, :, 0]
    onehot = (target[:, :, None] == jnp.arange(n_elem, dtype=jnp.int32)[None, None, :]).astype(
        jnp.int32
    )
    rank = jnp.sum((jnp.cumsum(onehot, axis=1) - 1) * onehot, axis=2)
    position = (
        (jnp.arange(groups, dtype=jnp.int32)[:, None] * n_elem + target) * slots + rank
    ).reshape(-1)
    buffer_size = groups * n_elem * slots
    elem_buf = (
        jnp.full((buffer_size,), -1, jnp.int32)
        .at[position]
        .set(local_elem.reshape(-1))
        .reshape(groups * n_elem, slots)
    )
    steps_x_buf = (
        jnp.zeros((buffer_size,), jnp.int32)
        .at[position]
        .set(lattice[:, 0, :].reshape(-1))
        .reshape(groups * n_elem, slots)
    )
    steps_y_buf = (
        jnp.zeros((buffer_size,), jnp.int32)
        .at[position]
        .set(lattice[:, 1, :].reshape(-1))
        .reshape(groups * n_elem, slots)
    )
    payload = interpolate(
        (
            lax.all_to_all(elem_buf, ("frame", "elem"), split_axis=0, concat_axis=0, tiled=True),
            lax.all_to_all(steps_x_buf, ("frame", "elem"), split_axis=0, concat_axis=0, tiled=True),
            lax.all_to_all(steps_y_buf, ("frame", "elem"), split_axis=0, concat_axis=0, tiled=True),
        ),
        table_db,
        elem_count,
    )
    returned = lax.all_to_all(payload, ("frame", "elem"), split_axis=0, concat_axis=0, tiled=True)
    flat_returned = returned.reshape((buffer_size,) + returned.shape[2:])
    picked = jnp.take(flat_returned, position, axis=0).reshape((groups, cells) + returned.shape[2:])
    spectra = transform(picked)
    source_spec = jnp.take(spectra, pair_source, axis=0)
    receiver_spec = jnp.take(spectra, pair_receiver + groups // 2, axis=0)
    product = jnp.einsum(
        "pnck,pnck->pnk", source_spec, receiver_spec, preferred_element_type=jnp.float32
    )
    cross = product[:, :, :NF] + product[:, :, NF:]
    kernel = jnp.einsum("fk,pnk->pfn", filters, cross, precision=lax.Precision.HIGHEST)
    return kernel / math.sqrt(NF)


def solution(mesh):
    placed = (
        P("frame", "elem", None, None, None),
        P(None, ("frame", "elem"), None),
        P(None, ("frame", "elem")),
        P(None, None, ("frame", "elem")),
        P(),
        P(),
        P(),
    )
    return jax.shard_map(
        local,
        mesh=mesh,
        in_specs=placed,
        out_specs=P(None, None, ("frame", "elem")),
        check_vma=False,
    )
```

profile of v0, /device:TPU:1, one launch (start us, length us, event | category | flops | bytes accessed | tf_op | source)
XLA Modules:
  0.0 245.6 jit_solution(6718673722219970499)
XLA Ops:
  0.0 0.8 copy.34
  0.8 2.5 %select_reduce_fusion = s32[8,128]{0,1:T(8,128)S(1)} fusion(s32[8,128]{0,1:T(8,128)S(1)} %copy.34), kind=kOutput, calls=%fused_computation.19 | output fusion | flops 2178048 | bytes 8192 | tf_op jit(solution)/shard_map/jit(cumsum)/reduce_window_sum | solution.py:76
  3.4 0.8 fusion.31
  4.2 0.1 add.286
  4.3 0.7 compare_select_fusion
  5.0 4.3 %scatter_custom_fusion.1 = s32[1536]{0:T(1024)S(1)} fusion(s32[1024]{0:T(1024)S(1)} %bitcast.47, s32[1024]{0:T(1024)S(1)} %bitcast.53, s32[]{:T(128)} %constant.137.clone.1), kind=kCustom, calls=%fused_computation.67 | custom fusion | bytes 6148 | tf_op jit(solution)/shard_map/scatter | solution.py:90
  9.3 0.7 all_to_all.23
  10.0 11.5 %all-to-all-start.1 = ((s32[128,1,12]{2,1,0:T(1,128)}), s32[128,1,12]{2,1,0:T(1,128)S(1)}, u32[]{:S(2)}, u32[]{:S(2)}) async-start(s32[128,1,12]{2,1,0:T(1,128)} %bitcast.10), calls=%async_computation.1 | async-start | bytes 131072 | tf_op jit(solution)/shard_map/all_to_all | solution.py:102
  21.5 4.3 %scatter_custom_fusion.2 = s32[1536]{0:T(1024)S(1)} fusion(s32[1024]{0:T(1024)S(1)} %bitcast.48, s32[1024]{0:T(1024)S(1)} %bitcast.52, s32[]{:T(128)} %constant.137.clone.1), kind=kCustom, calls=%fused_computation.65 | custom fusion | bytes 6148 | tf_op jit(solution)/shard_map/scatter | solution.py:96
  25.8 0.7 all_to_all.25
  26.6 4.5 %all-to-all-done.1 = s32[128,1,12]{2,1,0:T(1,128)S(1)} async-done(((s32[128,1,12]{2,1,0:T(1,128)}), s32[128,1,12]{2,1,0:T(1,128)S(1)}, u32[]{:S(2)}, u32[]{:S(2)}) %all-to-all-start.1) | async-done | bytes 6176 | tf_op jit(solution)/shard_map/all_to_all | solution.py:102
  31.0 5.3 %all-to-all-start.2 = ((s32[128,1,12]{2,1,0:T(1,128)}), s32[128,1,12]{2,1,0:T(1,128)S(1)}, u32[]{:S(2)}, u32[]{:S(2)}) async-start(s32[128,1,12]{2,1,0:T(1,128)} %bitcast.12), calls=%async_computation.2 | async-start | bytes 131072 | tf_op jit(solution)/shard_map/all_to_all | solution.py:103
  36.3 4.5 %scatter_custom_fusion = s32[1536]{0:T(1024)S(1)} fusion(s32[1024]{0:T(1024)S(1)} %bitcast.49, s32[1024]{0:T(1024)} %bitcast.54, s32[]{:T(128)} %constant.138.clone.1), kind=kCustom, calls=%fused_computation.69 | custom fusion | bytes 6656 | tf_op jit(solution)/shard_map/scatter | solution.py:84
  40.8 0.7 all_to_all.21
  41.5 13.5 %copy.40 = bf16[1,128,25,6,256]{4,3,2,1,0:T(8,128)(2,1)S(1)} copy(bf16[1,128,25,6,256]{4,1,3,2,0:T(8,128)(2,1)} %param.9) | data formatting | bytes 19660800 | tf_op args[0]
  55.1 6.5 %copy.56 = bf16[400,8,6,256]{3,1,2,0:T(8,128)(2,1)} copy(bf16[400,8,6,256]{3,2,1,0:T(8,128)(2,1)S(1)} %bitcast.41) | data formatting | bytes 19660800
  61.6 9.8 %all-to-all-start = ((s32[128,1,12]{2,1,0:T(1,128)}), s32[128,1,12]{2,1,0:T(1,128)S(1)}, u32[]{:S(2)}, u32[]{:S(2)}) async-start(s32[128,1,12]{2,1,0:T(1,128)} %bitcast.8), calls=%async_computation | async-start | bytes 131072 | tf_op jit(solution)/shard_map/all_to_all | solution.py:101
  71.4 1.5 multiply_reduce_fusion
  72.8 0.1 div.152
  72.9 0.1 div.159
  73.1 0.1 div.168
  73.2 0.1 div.174
  73.3 0.1 div.178
  73.4 0.1 div.184
  73.5 0.1 div.192
  73.6 0.1 div.197
  74.1 6.8 %all-to-all-done = s32[128,1,12]{2,1,0:T(1,128)S(1)} async-done(((s32[128,1,12]{2,1,0:T(1,128)}), s32[128,1,12]{2,1,0:T(1,128)S(1)}, u32[]{:S(2)}, u32[]{:S(2)}) %all-to-all-start) | async-done | bytes 6176 | tf_op jit(solution)/shard_map/all_to_all | solution.py:101
  80.9 0.5 broadcast.850
  81.4 0.8 reduce.37
  82.2 0.1 eq.37
  82.4 5.4 %broadcast_multiply_fusion = bf16[1536,128,25]{0,2,1:T(8,128)(2,1)} fusion(bf16[1536,25]{0,1:T(8,128)(2,1)S(1)} %convert_element_type.91, bf16[1536,128]{0,1:T(8,128)(2,1)S(1)} %fusion.7), kind=kLoop, calls=%fused_computation.9 | loop fusion | flops 4915200 | bytes 10300416 | tf_op jit(solution)/shard_map/mul | solution.py:60
  87.8 14.5 %mul.463 = bf16[1536,3200]{0,1:T(8,128)(2,1)} reshape(bf16[1536,128,25]{0,2,1:T(8,128)(2,1)} %broadcast_multiply_fusion) | data formatting | bytes 19660800 | tf_op jit(solution)/shard_map/mul | solution.py:60
  102.2 22.2 %convolution_convert_fusion = bf16[1536,1536]{1,0:T(8,128)(2,1)} fusion(bf16[1536,3200]{0,1:T(8,128)(2,1)} %mul.463, bf16[3200,1536]{1,0:T(8,128)(2,1)} %bitcast.42), kind=kOutput, calls=%fused_computation.6 | convolution fusion | flops 15101853696 | bytes 24379392 | tf_op jit(solution)/shard_map/dot_general | solution.py:61
  124.5 10.3 %reshape.461 = bf16[128,12,6,256]{3,2,1,0:T(8,128)(2,1)} reshape(bf16[1536,1536]{1,0:T(8,128)(2,1)} %convolution_convert_fusion) | data formatting | bytes 9437184 | tf_op jit(solution)/shard_map/reshape | solution.py:62
  134.8 5.7 %all-to-all-start.3 = ((bf16[128,12,6,256]{3,2,1,0:T(8,128)(2,1)}), bf16[128,12,6,256]{3,2,1,0:T(8,128)(2,1)}, u32[]{:S(2)}, u32[]{:S(2)}) async-start(bf16[128,12,6,256]{3,2,1,0:T(8,128)(2,1)} %reshape.461), calls=%async_computation.3 | async-start | bytes 12582912 | tf_op jit(solution)/shard_map/all_to_all | solution.py:108
  140.6 0.3 negate_multiply_fusion
  140.9 0.1 compare_and_fusion
  141.0 75.6 %all-to-all-done.3 = bf16[128,12,6,256]{3,2,1,0:T(8,128)(2,1)} async-done(((bf16[128,12,6,256]{3,2,1,0:T(8,128)(2,1)}), bf16[128,12,6,256]{3,2,1,0:T(8,128)(2,1)}, u32[]{:S(2)}, u32[]{:S(2)}) %all-to-all-start.3) | async-done | bytes 4718624 | tf_op jit(solution)/shard_map/all_to_all | solution.py:108
  216.6 11.0 %gather_fusion = bf16[1024,6,256]{2,1,0:T(8,128)(2,1)} fusion(bf16[1536,6,256]{2,1,0:T(8,128)(2,1)} %bitcast.13, s32[1024]{0:T(1024)S(1)} %broadcast_clamp_fusion), kind=kCustom, calls=%fused_computation.2 | custom fusion | bytes 6295552 | tf_op jit(solution)/shard_map/jit(_take)/gather | solution.py:110
  227.6 2.8 %copy.41 = bf16[1024,6,256]{2,0,1:T(8,128)(2,1)S(1)} copy(bf16[1024,6,256]{2,1,0:T(8,128)(2,1)} %gather_fusion) | data formatting | bytes 6291456 | tf_op jit(solution)/shard_map/jit(_take)/gather | solution.py:110
  230.4 2.7 %fusion.3 = bf16[8,128,6,128]{3,1,2,0:T(8,128)(2,1)S(1)} fusion(f32[256,64]{0,1:T(8,128)S(1)} %get-tuple-element.34, f32[256,64]{0,1:T(8,128)S(1)} %get-tuple-element.35, bf16[8,128,6,256]{3,1,0,2:T(8,128)(2,1)S(1)} %bitcast.43, pred[8,128]{1,0:T(8,128)(4,1)S(1)} %compare_and_fusion), kind=kOutput, calls=%fused_computation.13 | convolution fusion | flops 2418311168 | bytes 4850688 | tf_op jit(solution)/shard_map/dot_general | solution.py:47
  233.1 2.6 %gather_fusion.2 = bf16[16,128,6,128]{3,1,2,0:T(8,128)(2,1)} fusion(bf16[8,128,6,128]{3,1,2,0:T(8,128)(2,1)S(1)} %fusion.3, s32[1024]{0:T(1024)S(1)} %pad_clamp_fusion), kind=kCustom, calls=%fused_computation.1.clone | custom fusion | bytes 6291520 | tf_op jit(solution)/shard_map/jit(_take)/gather | solution.py:113
  235.7 2.6 %gather_fusion.1 = bf16[16,128,6,128]{3,1,2,0:T(8,128)(2,1)} fusion(bf16[8,128,6,128]{3,1,2,0:T(8,128)(2,1)S(1)} %fusion.3, s32[1024]{0:T(1024)S(1)} %pad_clamp_fusion.1), kind=kCustom, calls=%fused_computation.clone | custom fusion | bytes 6291520 | tf_op jit(solution)/shard_map/jit(_take)/gather | solution.py:112
  238.4 4.8 %fusion = f32[16,128,128]{2,1,0:T(8,128)S(1)} fusion(bf16[16,128,6,128]{3,1,2,0:T(8,128)(2,1)} %gather_fusion.2, bf16[16,128,6,128]{3,1,2,0:T(8,128)(2,1)} %gather_fusion.1, pred[16]{0:T(512)(128)(4,1)S(1)} %get-tuple-element.14, pred[16]{0:T(512)(128)(4,1)S(1)} %get-tuple-element.36), kind=kLoop, calls=%fused_computation.8 | loop fusion | flops 9175040 | bytes 7340064
  243.2 0.4 fusion.30
  243.5 0.3 copy.54
  243.8 0.3 copy.55
  244.2 1.4 fusion.6
  (23 shorter events, 0.5 us)
Async XLA Ops:
  0.0 244.2 %copy-start = (f32[64,64]{1,0:T(8,128)S(1)}, f32[64,64]{1,0:T(8,128)}, u32[]{:S(2)}) copy-start(f32[64,64]{1,0:T(8,128)} %param.15) | copy-start | bytes 49156
  10.0 21.0 %all-to-all-start.1 = ((s32[128,1,12]{2,1,0:T(1,128)}), s32[128,1,12]{2,1,0:T(1,128)S(1)}, u32[]{:S(2)}, u32[]{:S(2)}) async-start(s32[128,1,12]{2,1,0:T(1,128)} %bitcast.10), calls=%async_computation.1 | async-start | bytes 131072 | tf_op jit(solution)/shard_map/all_to_all | solution.py:102
  31.0 30.5 %all-to-all-start.2 = ((s32[128,1,12]{2,1,0:T(1,128)}), s32[128,1,12]{2,1,0:T(1,128)S(1)}, u32[]{:S(2)}, u32[]{:S(2)}) async-start(s32[128,1,12]{2,1,0:T(1,128)} %bitcast.12), calls=%async_computation.2 | async-start | bytes 131072 | tf_op jit(solution)/shard_map/all_to_all | solution.py:103
  61.6 19.3 %all-to-all-start = ((s32[128,1,12]{2,1,0:T(1,128)}), s32[128,1,12]{2,1,0:T(1,128)S(1)}, u32[]{:S(2)}, u32[]{:S(2)}) async-start(s32[128,1,12]{2,1,0:T(1,128)} %bitcast.8), calls=%async_computation | async-start | bytes 131072 | tf_op jit(solution)/shard_map/all_to_all | solution.py:101
  134.8 5.7 %copy-start.2 = (s32[16]{0:T(128)S(1)}, s32[16]{0:T(128)}, u32[]{:S(2)}) copy-start(s32[16]{0:T(128)} %param.14) | copy-start | bytes 196
  134.8 5.7 %copy-start.3 = (s32[16]{0:T(128)S(1)}, s32[16]{0:T(128)}, u32[]{:S(2)}) copy-start(s32[16]{0:T(128)} %param.13) | copy-start | bytes 196
  134.8 6.1 %copy-start.1 = (s32[8,128,1]{1,2,0:T(1,128)S(1)}, s32[8,128,1]{1,2,0:T(1,128)}, u32[]{:S(2)}) copy-start(s32[8,128,1]{1,2,0:T(1,128)} %param.10) | copy-start | bytes 12292
  134.8 81.8 %all-to-all-start.3 = ((bf16[128,12,6,256]{3,2,1,0:T(8,128)(2,1)}), bf16[128,12,6,256]{3,2,1,0:T(8,128)(2,1)}, u32[]{:S(2)}, u32[]{:S(2)}) async-start(bf16[128,12,6,256]{3,2,1,0:T(8,128)(2,1)} %reshape.461), calls=%async_computation.3 | async-start | bytes 12582912 | tf_op jit(solution)/shard_map/all_to_all | solution.py:108
where the time goes:
time: 247 us; the launch traced here: 246 us
  waiting for transfers between devices  86.9 us (35%)
  local copies, waits for them, and re-layouts  83.6 us (34%)
  starting transfers between devices  32.3 us (13%)
  matrix products  26.3 us (11%)
  other arithmetic  16.2 us (7%)
    all_to_all x1, waiting for transfers between devices, local(): lax.all_to_all(payload, ('frame', 'elem'), split_axis=0, concat_axis=0, t...  75.6 us
    dot_general x1, matrix products, interpolate(): jnp.dot(dense, table_db, preferred_element_type=jnp.float32)  22.2 us
    unnamed x12, local copies, waits for them, and re-layouts  20.7 us
    mul x1, local copies, waits for them, and re-layouts, interpolate(): hit[:, :, None] * weights[:, None, :]  14.5 us
    gather x2, local copies, waits for them, and re-layouts, local(): jnp.take(flat_returned, position, axis=0)  13.9 us
    all_to_all x1, starting transfers between devices, local(): lax.all_to_all(steps_x_buf, ('frame', 'elem'), split_axis=0, concat_axis=...  11.5 us
    reshape x1, local copies, waits for them, and re-layouts, interpolate(): trace = trace.reshape(shape + (C, T_SIZE))  10.3 us
    all_to_all x1, starting transfers between devices, local(): lax.all_to_all(elem_buf, ('frame', 'elem'), split_axis=0, concat_axis=0,...  9.77 us
  transfers between devices with their start and end apart: 4, of which 3 were waited for; matrix products, arithmetic and copies ran while one was open for 13% of the time, Pallas kernels for 0%

commit v1 on v0

v1 whole, which is shorter than its diff:
```python
import functools
import math

import jax
import jax.numpy as jnp
import ml_dtypes
import numpy as np
from jax import lax
from jax.experimental import pallas as pl
from jax.experimental.pallas import tpu as pltpu
from jax.sharding import PartitionSpec as P

C = 6
T = 256
NF = 64
Q = 64
NP = 25
E = 128
CELLS = 128
G = 8
NE = 16
DEV = G * NE
CAP = 12
PAIRS = 16
FILT = 64
ROWS = 24
WIDE = 384
UNROLL = 5
SPLIT = 2
BLOCK = 16
SLOTS = BLOCK * CAP
HALF = BLOCK // 2
ORDER = (0, 2, 4, 1, 3, 5)
MESH = pl.DeviceIdType.MESH

gll_nodes = [-1.0, -math.sqrt(3.0 / 7.0), 0.0, math.sqrt(3.0 / 7.0), 1.0]


def dft_table():
    phase = (np.arange(T)[:, None] * np.arange(NF)[None, :] % T) * (2.0 * math.pi / T)
    table = np.concatenate([np.cos(phase), -np.sin(phase)], axis=1) / math.sqrt(T)
    return table.astype(ml_dtypes.bfloat16)


def basis_rows():
    lane = lax.broadcasted_iota(jnp.int32, (1, 128), 1)
    rows = []
    for part in range(2):
        own = lane // 5 if part == 0 else lane % 5
        out = [jnp.zeros((1, 128), jnp.float32) for _ in range(5)]
        for i in range(5):
            others = [gll_nodes[m] for m in range(5) if m != i]
            scale = 1.0
            for node in others:
                scale *= gll_nodes[i] - node
            for k, value in enumerate(others + [1.0 / scale]):
                out[k] = jnp.where((own == i) & (lane < NP), value, out[k])
        rows += out
    return rows


def offset(block, dd):
    dy = (block + dd + dd // 4 + 1) % 4
    return (dd + 1) % 4, dy, (dd // 4 + 1) % 4, block // 4


SELF = 15
SELF_BLOCK = next(block for block in range(4) if offset(block, SELF) == (0, 0, 0, 0))


def slot_table():
    table = np.zeros((DEV // BLOCK, SLOTS, 128), np.float32)
    for block in range(DEV // BLOCK):
        for dd in range(BLOCK):
            dx, dy, dz, dc = offset(block, dd)
            for j in range(CAP):
                size = BLOCK if block else HALF
                part, at = divmod(dd, size)
                row = at * 8 + j if j < 8 else size * 8 + at * 4 + j - 8
                table[block, part * size * CAP + row, (dy * 2 + dc) * NE + dx * 4 + dz] = 1.0
    return table.astype(ml_dtypes.bfloat16)


def constants():
    return np.concatenate([dft_table(), slot_table().reshape(-1, 128)])


def iota(shape, dim):
    return lax.broadcasted_iota(jnp.int32, shape, dim)


def nt(a, b):
    return lax.dot_general(
        a, b, (((1,), (1,)), ((), ())), preferred_element_type=jnp.float32
    )


def nn(a, b):
    return jnp.dot(a, b, preferred_element_type=jnp.float32)


def kernel(
    db_hbm, owner_hbm, elem_hbm, lattice_hbm, source_hbm, receiver_hbm, filters_hbm, constants_hbm,
    out_hbm,
    owner_ref, elem_ref, lattice_ref, source_ref, receiver_ref, filters_ref, constants_ref,
    raw, db, asked, middle, wanted, dense_a, dense_b, send, recv, onehot, spectra, cross, result,
    small_sem, load_sem, ask_send, ask_recv, pass_send, pass_recv, ret_send, ret_recv, out_sem,
):
    me_f = lax.axis_index("frame")
    me_e = lax.axis_index("elem")
    me = me_f * NE + me_e
    me_x, me_z = lax.div(me_e, 4), lax.rem(me_e, 4)

    me_y, me_c = lax.div(me_f, 2), lax.rem(me_f, 2)

    def frame_at(dy, dc):
        return lax.rem(me_y + (dy + 4), 4) * 2 + lax.rem(me_c + dc, 2)

    def elem_at(dx, dz):
        return lax.rem(me_x + (dx + 4), 4) * 4 + lax.rem(me_z + (dz + 4), 4)

    small = [
        pltpu.make_async_copy(src, dst, small_sem.at[k])
        for k, (src, dst) in enumerate(
            (
                (owner_hbm, owner_ref),
                (elem_hbm, elem_ref),
                (lattice_hbm, lattice_ref),
                (constants_hbm, constants_ref),
                (filters_hbm, filters_ref),
                (source_hbm, source_ref),
                (receiver_hbm, receiver_ref),
            )
        )
    ]
    for copy in small[:4]:
        copy.start()

    barrier = pltpu.get_barrier_semaphore()
    for k in range(1, G):
        pl.semaphore_signal(
            barrier, inc=1, device_id=(frame_at(k // 2, k % 2), me_e), device_id_type=MESH
        )
    for k in range(1, NE):
        pl.semaphore_signal(
            barrier, inc=1, device_id=(me_f, elem_at(k // 4, k % 4)), device_id_type=MESH
        )

    def load(p):
        return [
            pltpu.make_async_copy(
                db_hbm.at[p, :, :, pl.ds(half * 128, 128)], raw.at[p, half], load_sem.at[p]
            )
            for half in range(2)
        ]

    def start_load(p, carry):
        for copy in load(p):
            copy.start()
        return carry

    lax.fori_loop(0, NP, start_load, 0)
    for copy in small[4:]:
        copy.start()
    for copy in small[:3]:
        copy.wait()

    owner = owner_ref[...]
    columns = jnp.transpose(owner.astype(jnp.float32)).astype(jnp.int32)
    lane = iota((CELLS, CELLS), 1)
    sub = iota((CELLS, CELLS), 0)
    row16 = iota((16, CELLS), 0)
    for g in range(G):
        row = owner[g : g + 1, :]
        col = columns[:, g : g + 1]
        same = row == col
        rank = jnp.sum(jnp.where(same & (sub < lane), 1, 0), axis=0, keepdims=True)
        hot_e = jnp.where(row16 == row, 1.0, 0.0).astype(jnp.bfloat16)
        here = row16 == rank
        parts = [
            jnp.where(here, value.astype(jnp.float32), 0.0)
            for value in (
                elem_ref[g : g + 1, :] + 1,
                lattice_ref[2 * g : 2 * g + 1, :],
                lattice_ref[2 * g + 1 : 2 * g + 2, :],
            )
        ]
        parts.append(jnp.zeros((CELLS - 48, CELLS), jnp.float32))
        values = jnp.concatenate(parts, axis=0).astype(jnp.bfloat16)
        asked[g] = nt(hot_e, values).reshape(NE, 1, 128)

    pl.semaphore_wait(barrier, G - 1 + NE - 1)
    for k in range(1, G):
        to_f = frame_at(-(k // 2), k % 2)
        pltpu.make_async_remote_copy(
            src_ref=asked.at[to_f],
            dst_ref=middle.at[k],
            send_sem=ask_send,
            recv_sem=ask_recv,
            device_id=(to_f, me_e),
            device_id_type=MESH,
        ).start()
    pltpu.make_async_copy(asked.at[me_f], middle.at[0], ask_recv).start()

    small[3].wait()
    table = constants_ref[:T]

    def to_spectrum(step, carry):
        for k in range(UNROLL):
            at = raw.at[step * UNROLL + k]
            pltpu.make_async_copy(at, at, load_sem.at[step * UNROLL + k]).wait()
        for k in range(UNROLL):
            p = step * UNROLL + k
            halves = [raw[p, half].reshape(C * E, 128) for half in range(2)]
            value = nn(jnp.concatenate(halves, axis=1), table).astype(jnp.bfloat16)
            at = pl.multiple_of(p * E, E)
            for k, c in enumerate(ORDER):
                db[k, pl.ds(at, E), :] = value[c * E : (c + 1) * E, :]
        return carry

    lax.fori_loop(0, SPLIT, to_spectrum, 0)
    pltpu.make_async_copy(middle, middle, ask_recv).wait()
    for k in range(1, NE):
        to_e = elem_at(-(k // 4), -(k % 4))
        pltpu.make_async_remote_copy(
            src_ref=middle.at[:, to_e],
            dst_ref=wanted.at[:, k],
            send_sem=pass_send,
            recv_sem=pass_recv,
            device_id=(me_f, to_e),
            device_id_type=MESH,
        ).start()
    pltpu.make_async_copy(middle.at[:, me_e], wanted.at[:, 0], pass_recv).start()
    lax.fori_loop(SPLIT, NP // UNROLL, to_spectrum, 0)
    for copy in small[4:]:
        copy.wait()
    pltpu.make_async_copy(wanted, wanted, pass_recv).wait()

    def own_slots(size):
        r = iota((size * CAP, 128), 0)
        j_row = jnp.where(r < size * 8, r & 7, 8 + (r & 3))
        return (iota((size * CAP, 128), 1) & 15) == j_row

    spread = jnp.where((iota((128, WIDE), 0) >> 4) == (iota((128, WIDE), 1) >> 7), 1.0, 0.0).astype(jnp.bfloat16)
    lane_f = (iota((1, 128), 1) + 1).astype(jnp.float32)

    basis = basis_rows()
    wanted_rows = wanted[...].reshape(DEV, 128).astype(jnp.bfloat16)

    def weigh(first, size, dense):
        rows = pl.ds(pl.multiple_of(T + first * CAP, 32), size * CAP)
        rows = nn(constants_ref[rows, :], wanted_rows)
        rows = jnp.where(own_slots(size), rows, 0.0).astype(jnp.bfloat16)
        wide = nn(rows, spread)
        hit = wide[:, :128] == lane_f
        weight = None
        for part in range(2):
            coord = wide[:, 128 * (part + 1) : 128 * (part + 2)] * (2.0 / Q) - 1.0
            value = basis[part * 5 + 4]
            for k in range(4):
                value = value * (coord - basis[part * 5 + k])
            weight = value if weight is None else weight * value
        for p in range(NP):
            dense[p, : size * CAP] = jnp.where(hit, weight[:, p : p + 1], 0.0).astype(jnp.bfloat16)

    def interpolate(first, size, dense):
        lhs = jnp.concatenate([dense[p, : size * CAP] for p in range(NP)], axis=1)
        rhs = jnp.concatenate([db[k] for k in range(C)], axis=1)
        result = nn(lhs, rhs)
        low = iota((8, 128), 0) < 4
        for dd in range(size):
            parts = []
            for q in range(3):
                even = result[:, q * 128 : (q + 1) * 128]
                odd = result[:, WIDE + q * 128 : WIDE + (q + 1) * 128]
                parts += [even[dd * 8 : (dd + 1) * 8], odd[dd * 8 : (dd + 1) * 8]]
                at = size * 8 + (dd // 2) * 8
                even, odd = even[at : at + 8], odd[at : at + 8]
                if dd % 2 == 0:
                    parts.append(jnp.where(low, even, pltpu.roll(odd, 4, 0)))
                else:
                    parts.append(jnp.where(low, pltpu.roll(even, 4, 0), odd))
            send[first + dd] = jnp.concatenate(parts, axis=0).astype(jnp.bfloat16)

    def give(b, dd):
        dx, _, dz, _ = offset(0, dd)
        dy, dc = lax.rem(b + (dd + dd // 4 + 1), 4), lax.div(b, 4)
        pltpu.make_async_remote_copy(
            src_ref=send.at[b * BLOCK + dd],
            dst_ref=recv.at[me],
            send_sem=ret_send,
            recv_sem=ret_recv.at[me_f],
            device_id=(frame_at(dy, dc), elem_at(dx, dz)),
            device_id_type=MESH,
        ).start()

    def give_block(b):
        for dd in range(BLOCK):
            if dd == SELF:

                @pl.when(b != SELF_BLOCK)
                def _():
                    give(b, SELF)
            else:
                give(b, dd)

    for part, dense in enumerate((dense_a, dense_b)):
        weigh(part * HALF, HALF, dense)
        interpolate(part * HALF, HALF, dense)
        for dd in range(part * HALF, (part + 1) * HALF):
            give(0, dd)

    def two_blocks(i, carry):
        b = 2 * i + 1
        weigh((b + 1) * BLOCK, BLOCK, dense_b)
        interpolate(b * BLOCK, BLOCK, dense_a)
        give_block(b)
        weigh((b + 2) * BLOCK, BLOCK, dense_a)
        interpolate((b + 1) * BLOCK, BLOCK, dense_b)
        give_block(b + 1)
        return carry

    last = DEV // BLOCK - 1
    weigh(BLOCK, BLOCK, dense_a)
    lax.fori_loop(0, last // 2, two_blocks, 0)
    interpolate(last * BLOCK, BLOCK, dense_a)
    for dd in range(BLOCK):
        give(last, dd)
    pltpu.make_async_copy(send.at[SELF_BLOCK * BLOCK + SELF], recv.at[me], ret_recv.at[me_f]).start()

    wide_lane = iota((CELLS, WIDE), 1)
    for g in range(G):
        row = owner[g : g + 1, :]
        col = columns[:, g : g + 1]
        rank = jnp.sum(jnp.where((row == col) & (lane < sub), 1.0, 0.0), axis=1, keepdims=True).astype(jnp.int32)
        at_even = col * ROWS + jnp.where(rank < 8, rank, rank + 8)
        at_odd = col * ROWS + jnp.where(rank < 8, rank + 8, rank + 12)
        onehot[g, :CELLS] = jnp.where(wide_lane == at_even, 1.0, 0.0).astype(jnp.bfloat16)
        onehot[g, CELLS:] = jnp.where(wide_lane == at_odd, 1.0, 0.0).astype(jnp.bfloat16)

    for dc in range(2):
        groups = [frame_at(dy, dc) for dy in range(4)]
        for g in groups:
            block = recv.at[pl.ds(g * NE, NE)]
            pltpu.make_async_copy(block, block, ret_recv.at[g]).wait()
        for g in groups:
            rows = recv[pl.ds(g * NE, NE)].astype(jnp.float32)
            rows = [rows[:, q * ROWS : (q + 1) * ROWS].reshape(NE * ROWS, 128) for q in range(3)]
            spectra[g] = nn(onehot[g], jnp.concatenate(rows, axis=1).astype(jnp.bfloat16))

    def products(i, carry):
        at = pl.multiple_of(i * 8, 8)
        total = [None] * 16
        for half in range(2):
            for k in range(3):
                pieces = [
                    spectra[g, pl.ds(at + half * CELLS, 8), k * 128 : (k + 1) * 128] for g in range(G)
                ]
                for s in range(4):
                    for q in range(4):
                        term = pieces[s] * pieces[4 + q]
                        n = s * 4 + q
                        total[n] = term if total[n] is None else total[n] + term
        for n in range(16):
            cross[n, pl.ds(at, 8), :] = total[n]
        return carry

    lax.fori_loop(0, CELLS // 8, products, 0)

    bank = filters_ref[...] * (1.0 / math.sqrt(NF))
    bank = jnp.concatenate([bank, bank], axis=1)
    bank_high = bank.astype(jnp.bfloat16)
    bank_low = (bank - bank_high.astype(jnp.float32)).astype(jnp.bfloat16)
    bank = jnp.concatenate([bank_high, bank_low], axis=0)
    bank = jnp.concatenate([bank, bank], axis=1)

    for p in range(PAIRS):
        value = cross[source_ref[p] * 4 + receiver_ref[p]]
        high = value.astype(jnp.bfloat16)
        low = (value - high.astype(jnp.float32)).astype(jnp.bfloat16)
        both = nt(bank, jnp.concatenate([high, low], axis=1))
        result[p] = both[:FILT] + both[FILT:]
        pltpu.make_async_copy(result.at[p], out_hbm.at[p], out_sem).start()

    pltpu.make_async_copy(result, out_hbm, out_sem).wait()
    others = pl.ds(0, G - 1)
    pltpu.make_async_copy(asked.at[others], asked.at[others], ask_send).wait()
    others = pl.ds(0, NE - 1)
    pltpu.make_async_copy(middle.at[:, others], middle.at[:, others], pass_send).wait()
    others = pl.ds(0, DEV - 1)
    pltpu.make_async_copy(send.at[others], send.at[others], ret_send).wait()


def local(strain_db, owner, local_elem, lattice, pair_source, pair_receiver, filters):
    hbm = pl.BlockSpec(memory_space=pltpu.HBM)
    database = jnp.transpose(strain_db[0], (1, 2, 0, 3))
    return pl.pallas_call(
        kernel,
        out_shape=jax.ShapeDtypeStruct((PAIRS, FILT, CELLS), jnp.float32),
        in_specs=[hbm] * 8,
        out_specs=hbm,
        scratch_shapes=[
            pltpu.VMEM((G, CELLS), jnp.int32),
            pltpu.VMEM((G, CELLS), jnp.int32),
            pltpu.VMEM((2 * G, CELLS), jnp.int32),
            pltpu.SMEM((PAIRS,), jnp.int32),
            pltpu.SMEM((PAIRS,), jnp.int32),
            pltpu.VMEM((FILT, NF), jnp.float32),
            pltpu.VMEM((T + DEV * CAP, 128), jnp.bfloat16),
            pltpu.VMEM((NP, 2, C, E, 128), jnp.bfloat16),
            pltpu.VMEM((C, NP * E, 128), jnp.bfloat16),
            pltpu.VMEM((G, NE, 1, 128), jnp.float32),
            pltpu.VMEM((G, NE, 1, 128), jnp.float32),
            pltpu.VMEM((G, NE, 1, 128), jnp.float32),
            pltpu.VMEM((NP, SLOTS, 128), jnp.bfloat16),
            pltpu.VMEM((NP, SLOTS, 128), jnp.bfloat16),
            pltpu.VMEM((DEV, 3 * ROWS, 128), jnp.bfloat16),
            pltpu.VMEM((DEV, 3 * ROWS, 128), jnp.bfloat16),
            pltpu.VMEM((G, 2 * CELLS, WIDE), jnp.bfloat16),
            pltpu.VMEM((G, 2 * CELLS, WIDE), jnp.float32),
            pltpu.VMEM((16, CELLS, 128), jnp.float32),
            pltpu.VMEM((PAIRS, FILT, CELLS), jnp.float32),
            pltpu.SemaphoreType.DMA((7,)),
            pltpu.SemaphoreType.DMA((NP,)),
            pltpu.SemaphoreType.DMA,
            pltpu.SemaphoreType.DMA,
            pltpu.SemaphoreType.DMA,
            pltpu.SemaphoreType.DMA,
            pltpu.SemaphoreType.DMA,
            pltpu.SemaphoreType.DMA((G,)),
            pltpu.SemaphoreType.DMA,
        ],
        compiler_params=pltpu.CompilerParams(
            collective_id=0, has_side_effects=True, vmem_limit_bytes=60 * 2**20
        ),
    )(
        database,
        owner.reshape(G, CELLS),
        local_elem,
        lattice.reshape(2 * G, CELLS),
        pair_source,
        pair_receiver,
        filters,
        jnp.asarray(constants()),
    )


def solution(mesh):
    placed = (
        P("frame", "elem", None, None, None),
        P(None, ("frame", "elem"), None),
        P(None, ("frame", "elem")),
        P(None, None, ("frame", "elem")),
        P(),
        P(),
        P(),
    )
    return jax.shard_map(
        local,
        mesh=mesh,
        in_specs=placed,
        out_specs=P(None, None, ("frame", "elem")),
        check_vma=False,
    )
```

time: 247 us -> 52.4 us (0.21)
  waiting for transfers between devices: 86.9 us -> 0 us
  local copies, waits for them, and re-layouts: 83.6 us -> 1.89 us
  Pallas kernels: 0 us -> 50.4 us
  starting transfers between devices: 32.3 us -> 0 us
  matrix products: 26.3 us -> 0 us
  other arithmetic: 16.2 us -> 0 us
    all_to_all x4 -> x0, waiting for transfers between devices: 86.9 us -> none  [the longest x1 75.6 us: local(): lax.all_to_all(payload, ('frame', 'elem'), split_axis=0, concat_axis=0, t...]
    pallas_call x0 -> x1, Pallas kernels: none -> 50.4 us  [local(): pl.pallas_call(kernel, out_shape=jax.ShapeDtypeStruct((PAIRS, FILT, CELLS...]
    all_to_all x4 -> x0, starting transfers between devices: 32.3 us -> none  [the longest x1 11.5 us: local(): lax.all_to_all(steps_x_buf, ('frame', 'elem'), split_axis=0, concat_axis=...]
    dot_general x3 -> x0, matrix products: 26.3 us -> none  [the longest x1 22.2 us: interpolate(): jnp.dot(dense, table_db, preferred_element_type=jnp.float32)]
    gather x4 -> x0, local copies, waits for them, and re-layouts: 19.1 us -> none  [the longest x2 13.9 us: local(): jnp.take(flat_returned, position, axis=0)]
    unnamed x12 -> x1, local copies, waits for them, and re-layouts: 20.7 us -> 1.89 us
    mul x1 -> x0, local copies, waits for them, and re-layouts: 14.5 us -> none  [interpolate(): hit[:, :, None] * weights[:, None, :]]
    scatter x3 -> x0, local copies, waits for them, and re-layouts: 13.1 us -> none  [the longest x1 4.48 us: local(): elem_buf = jnp.full((buffer_size,), -1, jnp.int32).at[position].set(local...]
  transfers between devices with their start and end apart: 4 -> 0, of which waited for: 3 -> 0; matrix products, arithmetic and copies ran while one was open for 13% -> 0% of each run, Pallas kernels for 0% -> 0%
where the time goes in v1:
time: 52.4 us; the launch traced here: 52.3 us
  Pallas kernels  50.4 us (96%)
  local copies, waits for them, and re-layouts  1.89 us (4%)
    pallas_call x1, Pallas kernels, local(): pl.pallas_call(kernel, out_shape=jax.ShapeDtypeStruct((PAIRS, FILT, CELLS...  50.4 us
    unnamed x1, local copies, waits for them, and re-layouts  1.89 us

profile of v1, /device:TPU:1, one launch (start us, length us, event | category | flops | bytes accessed | tf_op | source)
XLA Modules:
  0.0 52.3 jit_solution(11939550689783184268)
XLA Ops:
  0.0 50.4 %shard_map.82 = f32[16,64,128]{2,1,0:T(8,128)} custom-call(bf16[25,6,128,256]{3,2,1,0:T(8,128)(2,1)} %bitcast.5, s32[8,128]{1,0:T(8,128)} %bitcast.7, s32[8,128]{1,0:T(8,128)} %elem_hbm.1, s32[16,128]{1,0:T(8,128)} %bitcast.6, s32[16]{0:T(128)} %source_hbm.1, s32[16]{0:T(128)} %receiver_hbm.1, f32[64,64]{1,0:T(8,128)} %filters_hbm.1, ...), custom_call_target="tpu_custom_call" | custom-call | tf_op jit(solution)/shard_map/pallas_call | solution.py:397
  50.4 1.9 %copy.10 = f32[16,64,128]{2,1,0:T(8,128)} copy(f32[16,64,128]{2,1,0:T(8,128)} %shard_map.82) | data formatting | bytes 1048576

commit v2 on v1

--- a/solution.py
+++ b/solution.py
@@ -29,6 +29,7 @@
 SPLIT = 2
 BLOCK = 16
 SLOTS = BLOCK * CAP
+EARLY = 2
 HALF = BLOCK // 2
 ORDER = (0, 2, 4, 1, 3, 5)
 MESH = pl.DeviceIdType.MESH
@@ -74,7 +75,7 @@
         for dd in range(BLOCK):
             dx, dy, dz, dc = offset(block, dd)
             for j in range(CAP):
-                size = BLOCK if block else HALF
+                size = BLOCK if block >= EARLY else HALF
                 part, at = divmod(dd, size)
                 row = at * 8 + j if j < 8 else size * 8 + at * 4 + j - 8
                 table[block, part * size * CAP + row, (dy * 2 + dc) * NE + dx * 4 + dz] = 1.0
@@ -101,10 +102,10 @@
 
 def kernel(
     db_hbm, owner_hbm, elem_hbm, lattice_hbm, source_hbm, receiver_hbm, filters_hbm, constants_hbm,
-    out_hbm,
+    out_hbm, staged,
     owner_ref, elem_ref, lattice_ref, source_ref, receiver_ref, filters_ref, constants_ref,
-    raw, db, asked, middle, wanted, dense_a, dense_b, send, recv, onehot, spectra, cross, result,
-    small_sem, load_sem, ask_send, ask_recv, pass_send, pass_recv, ret_send, ret_recv, out_sem,
+    raw, db, asked, middle, wanted, dense_a, dense_b, dense_c, send, recv, onehot, spectra, cross, result,
+    small_sem, load_sem, ask_send, ask_recv, pass_send, pass_recv, ret_send, ret_recv, out_sem, stage_sem,
 ):
     me_f = lax.axis_index("frame")
     me_e = lax.axis_index("elem")
@@ -282,11 +283,11 @@
                     parts.append(jnp.where(low, pltpu.roll(even, 4, 0), odd))
             send[first + dd] = jnp.concatenate(parts, axis=0).astype(jnp.bfloat16)
 
-    def give(b, dd):
+    def give(b, dd, source=send):
         dx, _, dz, _ = offset(0, dd)
         dy, dc = lax.rem(b + (dd + dd // 4 + 1), 4), lax.div(b, 4)
         pltpu.make_async_remote_copy(
-            src_ref=send.at[b * BLOCK + dd],
+            src_ref=source.at[b * BLOCK + dd],
             dst_ref=recv.at[me],
             send_sem=ret_send,
             recv_sem=ret_recv.at[me_f],
@@ -294,38 +295,49 @@
             device_id_type=MESH,
         ).start()
 
-    def give_block(b):
-        for dd in range(BLOCK):
-            if dd == SELF:
-
-                @pl.when(b != SELF_BLOCK)
-                def _():
-                    give(b, SELF)
-            else:
-                give(b, dd)
-
-    for part, dense in enumerate((dense_a, dense_b)):
+    parts = EARLY * BLOCK // HALF
+    for part in range(parts):
+        dense = dense_a if part % 2 == 0 else dense_b
         weigh(part * HALF, HALF, dense)
+        if part == parts - 1:
+            weigh(EARLY * BLOCK, BLOCK, dense_c)
         interpolate(part * HALF, HALF, dense)
-        for dd in range(part * HALF, (part + 1) * HALF):
-            give(0, dd)
+        for index in range(part * HALF, (part + 1) * HALF):
+            if index != SELF_BLOCK * BLOCK + SELF:
+                give(index // BLOCK, index % BLOCK)
+
+    def staging(b):
+        second = pl.ds(b * BLOCK + HALF, HALF)
+        return pltpu.make_async_copy(send.at[second], staged.at[second], stage_sem.at[b])
+
+    def give_direct(b):
+        staging(b).start()
+        for dd in range(HALF):
+            give(b, dd)
+
+    def give_staged(b):
+        staging(b).wait()
+        for dd in range(HALF, BLOCK):
+            give(b, dd, staged)
 
     def two_blocks(i, carry):
-        b = 2 * i + 1
-        weigh((b + 1) * BLOCK, BLOCK, dense_b)
-        interpolate(b * BLOCK, BLOCK, dense_a)
-        give_block(b)
-        weigh((b + 2) * BLOCK, BLOCK, dense_a)
-        interpolate((b + 1) * BLOCK, BLOCK, dense_b)
-        give_block(b + 1)
+        b = 2 * i + EARLY
+        weigh((b + 1) * BLOCK, BLOCK, dense_a)
+        interpolate(b * BLOCK, BLOCK, dense_c)
+        give_direct(b)
+
+        @pl.when(i > 0)
+        def _():
+            give_staged(b - 1)
+
+        weigh(jnp.minimum(b + 2, DEV // BLOCK - 1) * BLOCK, BLOCK, dense_c)
+        interpolate((b + 1) * BLOCK, BLOCK, dense_a)
+        give_direct(b + 1)
+        give_staged(b)
         return carry
 
-    last = DEV // BLOCK - 1
-    weigh(BLOCK, BLOCK, dense_a)
-    lax.fori_loop(0, last // 2, two_blocks, 0)
-    interpolate(last * BLOCK, BLOCK, dense_a)
-    for dd in range(BLOCK):
-        give(last, dd)
+    lax.fori_loop(0, (DEV // BLOCK - EARLY) // 2, two_blocks, 0)
+    give_staged(DEV // BLOCK - 1)
     pltpu.make_async_copy(send.at[SELF_BLOCK * BLOCK + SELF], recv.at[me], ret_recv.at[me_f]).start()
 
     wide_lane = iota((CELLS, WIDE), 1)
@@ -394,11 +406,14 @@
 def local(strain_db, owner, local_elem, lattice, pair_source, pair_receiver, filters):
     hbm = pl.BlockSpec(memory_space=pltpu.HBM)
     database = jnp.transpose(strain_db[0], (1, 2, 0, 3))
-    return pl.pallas_call(
+    result, _ = pl.pallas_call(
         kernel,
-        out_shape=jax.ShapeDtypeStruct((PAIRS, FILT, CELLS), jnp.float32),
+        out_shape=[
+            jax.ShapeDtypeStruct((PAIRS, FILT, CELLS), jnp.float32),
+            jax.ShapeDtypeStruct((DEV, 3 * ROWS, 128), jnp.bfloat16),
+        ],
         in_specs=[hbm] * 8,
-        out_specs=hbm,
+        out_specs=[hbm, hbm],
         scratch_shapes=[
             pltpu.VMEM((G, CELLS), jnp.int32),
             pltpu.VMEM((G, CELLS), jnp.int32),
@@ -413,6 +428,7 @@
             pltpu.VMEM((G, NE, 1, 128), jnp.float32),
             pltpu.VMEM((G, NE, 1, 128), jnp.float32),
             pltpu.VMEM((NP, SLOTS, 128), jnp.bfloat16),
+            pltpu.VMEM((NP, HALF * CAP, 128), jnp.bfloat16),
             pltpu.VMEM((NP, SLOTS, 128), jnp.bfloat16),
             pltpu.VMEM((DEV, 3 * ROWS, 128), jnp.bfloat16),
             pltpu.VMEM((DEV, 3 * ROWS, 128), jnp.bfloat16),
@@ -429,6 +445,7 @@
             pltpu.SemaphoreType.DMA,
             pltpu.SemaphoreType.DMA((G,)),
             pltpu.SemaphoreType.DMA,
+            pltpu.SemaphoreType.DMA((DEV // BLOCK,)),
         ],
         compiler_params=pltpu.CompilerParams(
             collective_id=0, has_side_effects=True, vmem_limit_bytes=60 * 2**20
@@ -443,6 +460,7 @@
         filters,
         jnp.asarray(constants()),
     )
+    return result
 
 
 def solution(mesh):

time: 52.4 us -> 51.8 us (0.989)
  Pallas kernels: 50.4 us -> 49.8 us
    pallas_call x1, Pallas kernels: 50.4 us -> 49.8 us  [local(): pl.pallas_call(kernel, out_shape=[jax.ShapeDtypeStruct((PAIRS, FILT, CELL...]
where the time goes in v2:
time: 51.8 us; the launch traced here: 51.7 us
  Pallas kernels  49.8 us (96%)
  local copies, waits for them, and re-layouts  1.89 us (4%)
    pallas_call x1, Pallas kernels, local(): pl.pallas_call(kernel, out_shape=[jax.ShapeDtypeStruct((PAIRS, FILT, CELL...  49.8 us
    unnamed x1, local copies, waits for them, and re-layouts  1.89 us

profile of v2, /device:TPU:1, one launch (start us, length us, event | category | flops | bytes accessed | tf_op | source)
XLA Modules:
  0.0 51.7 jit_solution(8210243589849700269)
XLA Ops:
  0.0 49.8 %shard_map.82 = (f32[16,64,128]{2,1,0:T(8,128)}, bf16[128,72,128]{2,1,0:T(8,128)(2,1)}) custom-call(bf16[25,6,128,256]{3,2,1,0:T(8,128)(2,1)} %bitcast.5, s32[8,128]{1,0:T(8,128)} %bitcast.7, s32[8,128]{1,0:T(8,128)} %elem_hbm.1, s32[16,128]{1,0:T(8,128)} %bitcast.6, s32[16]{0:T(128)} %source_hbm.1, s32[16]{0:T(128)} %receiver_hbm.1, f32[64,64]{1,0:T(8,128)} %filters_hbm.1, ...), custom_call_target="tpu_custom_call" | custom-call | tf_op jit(solution)/shard_map/pallas_call | solution.py:409
  49.8 1.9 %copy.10 = f32[16,64,128]{2,1,0:T(8,128)} copy(f32[16,64,128]{2,1,0:T(8,128)} %get-tuple-element.6) | data formatting | bytes 1048576

commit v3 on v2

--- a/solution.py
+++ b/solution.py
@@ -102,10 +102,10 @@
 
 def kernel(
     db_hbm, owner_hbm, elem_hbm, lattice_hbm, source_hbm, receiver_hbm, filters_hbm, constants_hbm,
-    out_hbm, staged,
+    out_hbm,
     owner_ref, elem_ref, lattice_ref, source_ref, receiver_ref, filters_ref, constants_ref,
     raw, db, asked, middle, wanted, dense_a, dense_b, dense_c, send, recv, onehot, spectra, cross, result,
-    small_sem, load_sem, ask_send, ask_recv, pass_send, pass_recv, ret_send, ret_recv, out_sem, stage_sem,
+    small_sem, load_sem, ask_send, ask_recv, pass_send, pass_recv, ret_send, ret_recv, out_sem,
 ):
     me_f = lax.axis_index("frame")
     me_e = lax.axis_index("elem")
@@ -147,20 +147,12 @@
             barrier, inc=1, device_id=(me_f, elem_at(k // 4, k % 4)), device_id_type=MESH
         )
 
-    def load(p):
-        return [
+    for step in range(NP // UNROLL):
+        points = pl.ds(step * UNROLL, UNROLL)
+        for half in range(2):
             pltpu.make_async_copy(
-                db_hbm.at[p, :, :, pl.ds(half * 128, 128)], raw.at[p, half], load_sem.at[p]
-            )
-            for half in range(2)
-        ]
-
-    def start_load(p, carry):
-        for copy in load(p):
-            copy.start()
-        return carry
-
-    lax.fori_loop(0, NP, start_load, 0)
+                db_hbm.at[points, :, :, pl.ds(half * 128, 128)], raw.at[points, half], load_sem.at[step]
+            ).start()
     for copy in small[4:]:
         copy.start()
     for copy in small[:3]:
@@ -207,9 +199,8 @@
     table = constants_ref[:T]
 
     def to_spectrum(step, carry):
-        for k in range(UNROLL):
-            at = raw.at[step * UNROLL + k]
-            pltpu.make_async_copy(at, at, load_sem.at[step * UNROLL + k]).wait()
+        points = raw.at[pl.ds(step * UNROLL, UNROLL)]
+        pltpu.make_async_copy(points, points, load_sem.at[step]).wait()
         for k in range(UNROLL):
             p = step * UNROLL + k
             halves = [raw[p, half].reshape(C * E, 128) for half in range(2)]
@@ -283,11 +274,11 @@
                     parts.append(jnp.where(low, pltpu.roll(even, 4, 0), odd))
             send[first + dd] = jnp.concatenate(parts, axis=0).astype(jnp.bfloat16)
 
-    def give(b, dd, source=send):
+    def give(b, dd):
         dx, _, dz, _ = offset(0, dd)
         dy, dc = lax.rem(b + (dd + dd // 4 + 1), 4), lax.div(b, 4)
         pltpu.make_async_remote_copy(
-            src_ref=source.at[b * BLOCK + dd],
+            src_ref=send.at[b * BLOCK + dd],
             dst_ref=recv.at[me],
             send_sem=ret_send,
             recv_sem=ret_recv.at[me_f],
@@ -306,38 +297,19 @@
             if index != SELF_BLOCK * BLOCK + SELF:
                 give(index // BLOCK, index % BLOCK)
 
-    def staging(b):
-        second = pl.ds(b * BLOCK + HALF, HALF)
-        return pltpu.make_async_copy(send.at[second], staged.at[second], stage_sem.at[b])
-
-    def give_direct(b):
-        staging(b).start()
-        for dd in range(HALF):
-            give(b, dd)
-
-    def give_staged(b):
-        staging(b).wait()
-        for dd in range(HALF, BLOCK):
-            give(b, dd, staged)
-
     def two_blocks(i, carry):
         b = 2 * i + EARLY
         weigh((b + 1) * BLOCK, BLOCK, dense_a)
         interpolate(b * BLOCK, BLOCK, dense_c)
-        give_direct(b)
-
-        @pl.when(i > 0)
-        def _():
-            give_staged(b - 1)
-
+        for dd in range(BLOCK):
+            give(b, dd)
         weigh(jnp.minimum(b + 2, DEV // BLOCK - 1) * BLOCK, BLOCK, dense_c)
         interpolate((b + 1) * BLOCK, BLOCK, dense_a)
-        give_direct(b + 1)
-        give_staged(b)
+        for dd in range(BLOCK):
+            give(b + 1, dd)
         return carry
 
     lax.fori_loop(0, (DEV // BLOCK - EARLY) // 2, two_blocks, 0)
-    give_staged(DEV // BLOCK - 1)
     pltpu.make_async_copy(send.at[SELF_BLOCK * BLOCK + SELF], recv.at[me], ret_recv.at[me_f]).start()
 
     wide_lane = iota((CELLS, WIDE), 1)
@@ -377,7 +349,7 @@
             cross[n, pl.ds(at, 8), :] = total[n]
         return carry
 
-    lax.fori_loop(0, CELLS // 8, products, 0)
+    lax.fori_loop(0, CELLS // 8, products, 0, unroll=2)
 
     bank = filters_ref[...] * (1.0 / math.sqrt(NF))
     bank = jnp.concatenate([bank, bank], axis=1)
@@ -406,14 +378,11 @@
 def local(strain_db, owner, local_elem, lattice, pair_source, pair_receiver, filters):
     hbm = pl.BlockSpec(memory_space=pltpu.HBM)
     database = jnp.transpose(strain_db[0], (1, 2, 0, 3))
-    result, _ = pl.pallas_call(
+    return pl.pallas_call(
         kernel,
-        out_shape=[
-            jax.ShapeDtypeStruct((PAIRS, FILT, CELLS), jnp.float32),
-            jax.ShapeDtypeStruct((DEV, 3 * ROWS, 128), jnp.bfloat16),
-        ],
+        out_shape=jax.ShapeDtypeStruct((PAIRS, FILT, CELLS), jnp.float32),
         in_specs=[hbm] * 8,
-        out_specs=[hbm, hbm],
+        out_specs=hbm,
         scratch_shapes=[
             pltpu.VMEM((G, CELLS), jnp.int32),
             pltpu.VMEM((G, CELLS), jnp.int32),
@@ -437,7 +406,7 @@
             pltpu.VMEM((16, CELLS, 128), jnp.float32),
             pltpu.VMEM((PAIRS, FILT, CELLS), jnp.float32),
             pltpu.SemaphoreType.DMA((7,)),
-            pltpu.SemaphoreType.DMA((NP,)),
+            pltpu.SemaphoreType.DMA((NP // UNROLL,)),
             pltpu.SemaphoreType.DMA,
             pltpu.SemaphoreType.DMA,
             pltpu.SemaphoreType.DMA,
@@ -445,7 +414,6 @@
             pltpu.SemaphoreType.DMA,
             pltpu.SemaphoreType.DMA((G,)),
             pltpu.SemaphoreType.DMA,
-            pltpu.SemaphoreType.DMA((DEV // BLOCK,)),
         ],
         compiler_params=pltpu.CompilerParams(
             collective_id=0, has_side_effects=True, vmem_limit_bytes=60 * 2**20
@@ -460,7 +428,6 @@
         filters,
         jnp.asarray(constants()),
     )
-    return result
 
 
 def solution(mesh):

time: 51.8 us -> 51.6 us (level)
  no operation moved by 1% of the time
where the time goes in v3:
time: 51.6 us; the launch traced here: 51.5 us
  Pallas kernels  49.6 us (96%)
  local copies, waits for them, and re-layouts  1.89 us (4%)
    pallas_call x1, Pallas kernels, local(): pl.pallas_call(kernel, out_shape=jax.ShapeDtypeStruct((PAIRS, FILT, CELLS...  49.6 us
    unnamed x1, local copies, waits for them, and re-layouts  1.89 us

profile of v3, /device:TPU:1, one launch (start us, length us, event | category | flops | bytes accessed | tf_op | source)
XLA Modules:
  0.0 51.5 jit_solution(16253761474306150134)
XLA Ops:
  0.0 49.6 %shard_map.82 = f32[16,64,128]{2,1,0:T(8,128)} custom-call(bf16[25,6,128,256]{3,2,1,0:T(8,128)(2,1)} %bitcast.5, s32[8,128]{1,0:T(8,128)} %bitcast.7, s32[8,128]{1,0:T(8,128)} %elem_hbm.1, s32[16,128]{1,0:T(8,128)} %bitcast.6, s32[16]{0:T(128)} %source_hbm.1, s32[16]{0:T(128)} %receiver_hbm.1, f32[64,64]{1,0:T(8,128)} %filters_hbm.1, ...), custom_call_target="tpu_custom_call" | custom-call | tf_op jit(solution)/shard_map/pallas_call | solution.py:381
  49.6 1.9 %copy.10 = f32[16,64,128]{2,1,0:T(8,128)} copy(f32[16,64,128]{2,1,0:T(8,128)} %shard_map.82) | data formatting | bytes 1048576
